TPU v7x, 256 devices: a whole 4x4x8 slice. The times are simulated.
256 devices in a mesh: group: 8 (over z), ctx: 4 (over x_lo, core), head: 8 (over y, x_hi).
Axes of the slice: x: 4 (x_hi: 2, x_lo: 2; x = x_hi * 2 + x_lo), y: 4, z: 8, core: 2. Of those that a mesh axis runs over, the one named last changes fastest.
Arguments:
- prompt_q: bfloat16 [4096, 8192], P(('group', 'ctx'), 'head'), may hold values from -120 to 120
- prompt_kv: bfloat16 [2, 4096, 1024], P(None, ('group', 'ctx'), 'head'), may hold values from -4 to 4
- cont_q: bfloat16 [32, 256, 8192], P(('group', 'ctx'), None, 'head'), may hold values from -120 to 120
- cont_kv: bfloat16 [2, 32, 256, 1024], P(None, ('group', 'ctx'), None, 'head'), may hold values from -4 to 4
- cont_len: int32 [32], P(('group', 'ctx')), may hold values from 1 to 256, 4096 in all
Outputs:
- prompt_out: bfloat16 [4096, 8192], P(('group', 'ctx', 'head'))
- cont_out: bfloat16 [32, 256, 8192], P(('group', 'ctx'), 'head')
Inputs may be any that keep to these rules, and one draw needn't show every extreme that they name: The live positions of continuation c are its first cont_len[c] slots.
All inputs are finite; a program needn't handle non-finite values. No bound on the sum of `cont_len` on one device may be relied on, other than what follows from the above.
Results may differ from a plain program's by a relative error of at most 0.009.
Values may be sent and summed in bfloat16 or wider, within the bound.
No kernel may reach another device: no remote copies, remote signals or barrier semaphores. Data moves between devices by JAX's collectives and lax.ppermute only.
A program may use at most 128 MiB of HBM per device.

v0:
```python
import functools

import jax
import jax.numpy as jnp
from jax import lax
from jax.experimental import pallas as pl
from jax.experimental.pallas import tpu as pltpu
from jax.sharding import PartitionSpec as P

HD = 128
GQA = 8
ROWS_P = 128
ROWS_C = 256
ROWS = ROWS_P + ROWS_C
SLAB = 512
BLOCK = 128
LOW = -1e30
SCALE = HD**-0.5 * 1.4426950408889634
ROOM = 64 / SCALE

C_CORE = [(0, 1), (1, 0), (2, 3), (3, 2)]
C_X = [(0, 2), (2, 0), (1, 3), (3, 1)]
C_DIAG = [(0, 3), (3, 0), (1, 2), (2, 1)]


def weigh(q, keys, values, m, l, acc, mask=None):
    s = lax.dot_general(q, keys, (((1,), (1,)), ((), ())), preferred_element_type=jnp.float32)
    parts = [s[:, j : j + HD] for j in range(0, s.shape[1], HD)]
    if mask is not None:
        parts = [mask(j, part) for j, part in enumerate(parts)]
    m_new = jnp.maximum(m, jnp.max(functools.reduce(jnp.maximum, parts), axis=1, keepdims=True))
    alpha = jnp.exp2((m - m_new) * SCALE)
    l, acc = add(parts, values, m_new, l * alpha, acc * alpha)
    return m_new, l, acc


def weigh_kept(q, keys, values, m, l, acc, over, mask=None):
    s = lax.dot_general(q, keys, (((1,), (1,)), ((), ())), preferred_element_type=jnp.float32)
    parts = [s[:, j : j + HD] for j in range(0, s.shape[1], HD)]
    if mask is not None:
        parts = [mask(j, part) for j, part in enumerate(parts)]
    over = jnp.maximum(over, functools.reduce(jnp.maximum, parts) - m)
    return m, *add(parts, values, m, l, acc), over


def add(parts, values, m, l, acc):
    shift = m * SCALE
    p = jnp.concatenate([jnp.exp2(part * SCALE - shift).astype(jnp.bfloat16) for part in parts], axis=1)
    pv = jnp.dot(p, values, preferred_element_type=jnp.float32)
    return l + pv[:, HD:], acc + pv[:, :HD]


def fresh():
    zero = jnp.zeros((BLOCK, HD), jnp.float32)
    return zero + LOW, zero, zero


def extend(vx, values):
    vx[:, :HD] = values
    vx[:, HD:] = jnp.ones((vx.shape[0], HD), jnp.bfloat16)


def over_heads(together, fn, over):
    def some(i, over):
        for h in range(together):
            over = fn(i * together + h, over)
        return over

    return lax.fori_loop(0, GQA // together, some, over)


def columns(h):
    return pl.ds(h * HD if isinstance(h, int) else pl.multiple_of(h * HD, HD), HD)


def spread_kernel(live, out):
    out[...] = jnp.broadcast_to(live[...], out.shape)


def spread(live):
    return pl.pallas_call(
        spread_kernel,
        out_shape=jax.ShapeDtypeStruct((8, HD), jnp.int32),
        cost_estimate=pl.CostEstimate(flops=8 << 30, bytes_accessed=16 << 20, transcendentals=0),
        name="spread",
    )(live.reshape(1, 1))


def own_kernel(meta, qc, kv, m_out, l_out, acc_out, vx):
    extend(vx, kv[1, 0])
    for h in range(GQA):
        for r in (0, BLOCK):
            n = r + BLOCK

            def mask(j, part, r=r):
                row = r + lax.broadcasted_iota(jnp.int32, (BLOCK, HD), 0)
                col = j * HD + lax.broadcasted_iota(jnp.int32, (BLOCK, HD), 1)
                return jnp.where((col <= row) & (col < meta[0:1, :]), part, LOW)

            q = qc[0, r:n, columns(h)]
            at = pl.ds(ROWS_P + r, BLOCK)
            m_out[h, at, :], l_out[h, at, :], acc_out[h, at, :] = weigh(q, kv[0, 0, :n, :], vx[:n, :], *fresh(), mask)


def slab_kernel(n_slabs, step, last, *refs):
    meta, qp, qc = refs[:3]
    slabs = refs[3 : 3 + n_slabs]
    m_in, l_in, acc_in = refs[3 + n_slabs : 6 + n_slabs]
    n_out = 1 if last else 3
    outs = refs[6 + n_slabs : 6 + n_slabs + n_out]
    vxs, flag = refs[6 + n_slabs + n_out : -1], refs[-1]
    for vx, kv in zip(vxs, slabs):
        extend(vx, kv[1])

    ctx, z = lax.axis_index("ctx"), lax.axis_index("group")

    def own_mask(j, part):
        if j == 0:
            row = lax.broadcasted_iota(jnp.int32, (BLOCK, HD), 0)
            col = lax.broadcasted_iota(jnp.int32, (BLOCK, HD), 1)
            return jnp.where(col <= row, part, LOW)
        return jnp.where((ctx ^ j) < ctx, part, LOW)

    def run(h, r, running, over, partly=False):
        at = pl.ds(0 if r is None else ROWS_P + r, BLOCK)
        first = step == 0 and r is None
        state = fresh() if first else tuple(ref[h, at, :] for ref in (m_in, l_in, acc_in))
        q = qp[:, columns(h)] if r is None else qc[0, pl.ds(r, BLOCK), columns(h)]
        for i in range(n_slabs) if partly is not None else ():
            mask = own_mask if first else None
            if partly:
                mask = lambda j, part, i=i: jnp.where(sees[i], part, LOW)
            if running or first:
                state = weigh(q, slabs[i][0], vxs[i][...], *state, mask)
            else:
                *state, over = weigh_kept(q, slabs[i][0], vxs[i][...], *state, over, mask)
        if not last:
            if running or first:
                outs[0][h, at, :] = state[0]
            outs[1][h, at, :], outs[2][h, at, :] = state[1:]
            return over
        mixed = state[2] / state[1]
        if r is None:
            outs[0][:, :16, columns(h)] = mixed.reshape(8, 16, HD).astype(jnp.bfloat16)
        else:
            row = r + lax.broadcasted_iota(jnp.int32, (BLOCK, HD), 0)
            mixed = jnp.where(row < meta[0:1, :], mixed, 0.0).astype(jnp.bfloat16)
            outs[0][pl.ds(r // 32, BLOCK // 32), 16:, columns(h)] = mixed.reshape(BLOCK // 32, 32, HD)
        return over

    way = 2 * (ctx & 1) - 1
    sees = [jnp.bool_(True)] if step == 0 else [((z + (1 - 2 * i) * way * step) & 7) < z for i in range(n_slabs)]
    none = jnp.zeros((BLOCK, HD), jnp.float32)

    def rows(blocks, running=False, partly=False):
        def head(h, over):
            for r in blocks:
                over = run(h, r, running, over, partly)
            return over

        return over_heads(1 if running else 4, head, none)

    if step == 0:
        flag[...] = rows((None, 0, BLOCK))
    else:
        full = functools.reduce(jnp.logical_and, sees)
        some = functools.reduce(jnp.logical_or, sees)

        @pl.when(full)
        def _():
            flag[...] = rows((None, 0, BLOCK))

        @pl.when(jnp.logical_not(full))
        def _():
            flag[...] = rows((0, BLOCK))
            if n_slabs > 1:

                @pl.when(some)
                def _():
                    flag[...] = jnp.maximum(flag[...], rows((None,), partly=True))

            @pl.when(jnp.logical_not(some))
            def _():
                if last:
                    rows((None,), partly=None)
                else:
                    for before, after in ((l_in, outs[1]), (acc_in, outs[2])):
                        after[:, :ROWS_P, :] = before[:, :ROWS_P, :]

    @pl.when(jnp.max(flag[...]) > ROOM)
    def _():
        rows((0, BLOCK), running=True)
        rows((None,), running=True, partly=step != 0)


VMEM = pl.BlockSpec(memory_space=pltpu.VMEM)
ANY = pl.BlockSpec(memory_space=pl.ANY)
STATE = (jax.ShapeDtypeStruct((GQA, ROWS, HD), jnp.float32),) * 3
PARAMS = pltpu.CompilerParams(vmem_limit_bytes=32 << 20)


def cost(scores):
    return pl.CostEstimate(flops=scores * 512 * 2, bytes_accessed=1 << 20, transcendentals=scores)


def attend_own(meta, qc, kv):
    return pl.pallas_call(
        own_kernel,
        in_specs=[VMEM] * 3,
        out_specs=(VMEM,) * 3,
        out_shape=STATE,
        scratch_shapes=[pltpu.VMEM((ROWS_C, 2 * HD), jnp.bfloat16)],
        compiler_params=PARAMS,
        cost_estimate=cost(GQA * ROWS_C * ROWS_C),
        name="own",
    )(meta, qc, kv)


def attend(meta, qp, qc, slabs, state, step, last=False):
    n = len(slabs)
    if last:
        out_specs, alias = VMEM, {}
        out_shape = jax.ShapeDtypeStruct((8, 48, GQA * HD), jnp.bfloat16)
    else:
        out_specs, out_shape, alias = (VMEM,) * 3, STATE, {3 + n: 0}
    return pl.pallas_call(
        functools.partial(slab_kernel, n, step, last),
        in_specs=[VMEM] * (n + 6),
        out_specs=out_specs,
        out_shape=out_shape,
        input_output_aliases=alias,
        scratch_shapes=[pltpu.VMEM((SLAB, 2 * HD), jnp.bfloat16)] * n + [pltpu.VMEM((BLOCK, HD), jnp.float32)],
        compiler_params=PARAMS,
        cost_estimate=cost(GQA * ROWS * SLAB * n),
        name=f"slabs{step}",
    )(meta, qp, qc, *slabs, *state)


def lay_out_kernel(moved, prompt_out, cont_out, sems):
    copies = []
    for h in range(8):
        to = pl.ds(h * GQA * HD, GQA * HD)
        copies.append(pltpu.make_async_copy(moved.at[h, pl.ds(0, 16), :], prompt_out.at[:, to], sems.at[0, h]))
        copies.append(pltpu.make_async_copy(moved.at[h, pl.ds(16, 32), :], cont_out.at[0, :, to], sems.at[1, h]))
    for copy in copies:
        copy.start()
    for copy in copies:
        copy.wait()


def lay_out(moved):
    return pl.pallas_call(
        lay_out_kernel,
        in_specs=[ANY],
        out_specs=(ANY, ANY),
        out_shape=(
            jax.ShapeDtypeStruct((16, 8 * GQA * HD), jnp.bfloat16),
            jax.ShapeDtypeStruct((1, 32, 8 * GQA * HD), jnp.bfloat16),
        ),
        scratch_shapes=[pltpu.SemaphoreType.DMA((2, 8))],
        compiler_params=PARAMS,
        name="lay_out",
    )(moved)


def tie(*trees):
    return lax.optimization_barrier(trees)


def body(prompt_q, prompt_kv, cont_q, cont_kv, cont_len):
    n_z = 8
    ring = [(g * 4 + c, ((g + (1 if c % 2 == 0 else -1)) % n_z) * 4 + c) for g in range(n_z) for c in range(4)]

    def pass_on(x):
        return lax.ppermute(x, ("group", "ctx"), ring)

    def swap(x):
        return lax.ppermute(x, "ctx", C_CORE)

    meta = spread(cont_len)
    pieces = [lax.ppermute(prompt_kv, "ctx", pairs) for pairs in (C_CORE, C_X, C_DIAG)]
    state = attend_own(meta, cont_q, cont_kv)
    pieces, state = tie(pieces, state)
    own = jnp.concatenate([prompt_kv] + pieces, axis=1)

    near = pass_on(own)
    state = attend(meta, prompt_q, cont_q, [own], state, 0)
    near, state = tie(near, state)

    for step in (1, 2, 3):
        other = swap(near)
        coming = pass_on(near)
        state = attend(meta, prompt_q, cont_q, [near, other], state, step)
        near, state = tie(coming, state)
    mixed = attend(meta, prompt_q, cont_q, [near], state, 4, last=True)
    moved = lax.all_to_all(mixed, "head", split_axis=0, concat_axis=0, tiled=True)
    return lay_out(moved)


def solution(mesh):
    placed = (
        P(("group", "ctx"), "head"),
        P(None, ("group", "ctx"), "head"),
        P(("group", "ctx"), None, "head"),
        P(None, ("group", "ctx"), None, "head"),
        P(("group", "ctx")),
    )
    return jax.shard_map(
        body,
        mesh=mesh,
        in_specs=placed,
        out_specs=(P(("group", "ctx", "head"), None), P(("group", "ctx"), "head", None)),
        check_vma=False,
    )
```

profile of v0, /device:TPU:97, one launch (start us, length us, event | category | flops | bytes accessed | tf_op | source)
XLA Modules:
  0.0 93.6 jit_solution(5244452188425219337)
XLA Ops:
  0.6 1.3 %collective-permute-start.1 = (bf16[2,128,128]{2,1,0:T(8,128)(2,1)}, bf16[2,128,128]{2,1,0:T(8,128)(2,1)S(1)}, u32[]{:S(2)}, u32[]{:S(2)}) collective-permute-start(bf16[2,128,128]{2,1,0:T(8,128)(2,1)} %param.6), channel_id=1, source_target_pairs={{0,16},{16,0},{8,24},{24,8},{1,17},{17,1},{9,25},{25,9},{2,18},{18... | collective-permute-start | bytes 196616 | tf_op jit(solution)/shard_map/ppermute | solution.py:281
  1.9 1.0 %collective-permute-start = (bf16[2,128,128]{2,1,0:T(8,128)(2,1)}, bf16[2,128,128]{2,1,0:T(8,128)(2,1)S(1)}, u32[]{:S(2)}, u32[]{:S(2)}) collective-permute-start(bf16[2,128,128]{2,1,0:T(8,128)(2,1)} %param.6), channel_id=1, source_target_pairs={{0,8},{8,0},{16,24},{24,16},{1,9},{9,1},{17,25},{25,17},{2,10},{10... | collective-permute-start | bytes 196616 | tf_op jit(solution)/shard_map/ppermute | solution.py:281
  2.9 0.1 collective-permute-start.2
  3.7 0.0 copy-start.4
  3.7 0.0 copy-start
  3.7 0.0 copy-start.3
  3.7 0.7 spread.1.meta.refs_0_
  4.4 0.1 copy-done.4
  4.5 0.0 copy-start.1
  4.5 0.2 copy-done
  4.8 0.0 copy-done.3
  4.8 0.0 copy-start.2
  4.8 0.7 copy-done.2
  5.5 1.3 %own.1 = (f32[8,384,128]{2,1,0:T(8,128)S(1)}, f32[8,384,128]{2,1,0:T(8,128)S(1)}, f32[8,384,128]{2,1,0:T(8,128)S(1)}) custom-call(s32[8,128]{1,0:T(8,128)S(1)} %copy-done.2, bf16[1,256,1024]{2,1,0:T(8,128)(2,1)S(1)} %copy-done, bf16[2,1,256,128]{3,2,1,0:T(8,128)(2,1)S(1)} %copy-done.3), custom_call_target="tpu_custom_call" | custom-call | flops 536870912 | bytes 1048576 | tf_op jit(solution)/shard_map/own/pallas_call | solution.py:207
  6.8 0.0 collective-permute-done.1
  6.8 0.0 collective-permute-done
  6.8 0.0 collective-permute-done.2
  6.9 0.1 collective-permute-start.3
  7.0 0.0 copy-done.1
  7.0 11.6 %slabs0.1 = (f32[8,384,128]{2,1,0:T(8,128)S(1)}, f32[8,384,128]{2,1,0:T(8,128)S(1)}, f32[8,384,128]{2,1,0:T(8,128)S(1)}) custom-call(s32[8,128]{1,0:T(8,128)S(1)} %copy-done.2, bf16[128,1024]{1,0:T(8,128)(2,1)S(1)} %copy-done.1, bf16[1,256,1024]{2,1,0:T(8,128)(2,1)S(1)} %copy-done, ...), custom_call_target="tpu_custom_call", output_to_operand_aliasing={{0}: (4, {})} | custom-call | flops 1610612736 | bytes 1048576 | tf_op jit(solution)/shard_map/slabs0/pallas_call | solution.py:226
  18.6 0.0 collective-permute-done.3.refs_3_
  18.6 0.1 collective-permute-start.5
  18.7 2.2 %collective-permute-start.4 = (bf16[2,512,128]{2,1,0:T(8,128)(2,1)S(1)}, bf16[2,512,128]{2,1,0:T(8,128)(2,1)S(1)}, u32[]{:S(2)}, u32[]{:S(2)}) collective-permute-start(bf16[2,512,128]{2,1,0:T(8,128)(2,1)S(1)} %collective-permute-done.3.refs_3_), channel_id=1, source_target_pairs={{0,32},{8,232},{16,48},{24,248},{32,64},{40,8},{48,80},{56,24},{64... | collective-permute-start | bytes 786440 | tf_op jit(solution)/shard_map/ppermute | solution.py:275
  20.9 0.0 collective-permute-done.5.refs_4_
  20.9 14.9 %slabs1.1 = (f32[8,384,128]{2,1,0:T(8,128)S(1)}, f32[8,384,128]{2,1,0:T(8,128)S(1)}, f32[8,384,128]{2,1,0:T(8,128)S(1)}) custom-call(s32[8,128]{1,0:T(8,128)S(1)} %copy-done.2, bf16[128,1024]{1,0:T(8,128)(2,1)S(1)} %copy-done.1, bf16[1,256,1024]{2,1,0:T(8,128)(2,1)S(1)} %copy-done, ...), custom_call_target="tpu_custom_call", output_to_operand_aliasing={{0}: (5, {})} | custom-call | flops 3221225472 | bytes 1048576 | tf_op jit(solution)/shard_map/slabs1/pallas_call | solution.py:226
  35.8 0.0 collective-permute-done.4.refs_3_
  35.8 0.3 collective-permute-start.7
  36.1 0.1 collective-permute-start.6
  36.2 1.4 %collective-permute-done.7.refs_4_ = bf16[2,512,128]{2,1,0:T(8,128)(2,1)S(1)} collective-permute-done((bf16[2,512,128]{2,1,0:T(8,128)(2,1)S(1)}, bf16[2,512,128]{2,1,0:T(8,128)(2,1)S(1)}, u32[]{:S(2)}, u32[]{:S(2)}) %collective-permute-start.7) | collective-permute-done | bytes 262176 | tf_op jit(solution)/shard_map/ppermute | solution.py:278
  37.6 4.9 %slabs2.1 = (f32[8,384,128]{2,1,0:T(8,128)S(1)}, f32[8,384,128]{2,1,0:T(8,128)S(1)}, f32[8,384,128]{2,1,0:T(8,128)S(1)}) custom-call(s32[8,128]{1,0:T(8,128)S(1)} %copy-done.2, bf16[128,1024]{1,0:T(8,128)(2,1)S(1)} %copy-done.1, bf16[1,256,1024]{2,1,0:T(8,128)(2,1)S(1)} %copy-done, ...), custom_call_target="tpu_custom_call", output_to_operand_aliasing={{0}: (5, {})} | custom-call | flops 3221225472 | bytes 1048576 | tf_op jit(solution)/shard_map/slabs2/pallas_call | solution.py:226
  42.6 0.0 collective-permute-done.6.refs_3_
  42.6 10.1 %collective-permute-start.9 = (bf16[2,512,128]{2,1,0:T(8,128)(2,1)S(1)}, bf16[2,512,128]{2,1,0:T(8,128)(2,1)S(1)}, u32[]{:S(2)}, u32[]{:S(2)}) collective-permute-start(bf16[2,512,128]{2,1,0:T(8,128)(2,1)S(1)} %collective-permute-done.6.refs_3_), channel_id=1, source_target_pairs={{0,8},{8,0},{16,24},{24,16},{1,9},{9,1},{17,25},{25,17},{2,10},{10... | collective-permute-start | bytes 786440 | tf_op jit(solution)/shard_map/ppermute | solution.py:278
  52.8 1.4 %collective-permute-start.8 = (bf16[2,512,128]{2,1,0:T(8,128)(2,1)S(1)}, bf16[2,512,128]{2,1,0:T(8,128)(2,1)S(1)}, u32[]{:S(2)}, u32[]{:S(2)}) collective-permute-start(bf16[2,512,128]{2,1,0:T(8,128)(2,1)S(1)} %collective-permute-done.6.refs_3_), channel_id=1, source_target_pairs={{0,32},{8,232},{16,48},{24,248},{32,64},{40,8},{48,80},{56,24},{64... | collective-permute-start | bytes 786440 | tf_op jit(solution)/shard_map/ppermute | solution.py:275
  54.2 0.0 collective-permute-done.9.refs_4_
  54.2 15.1 %slabs3.1 = (f32[8,384,128]{2,1,0:T(8,128)S(1)}, f32[8,384,128]{2,1,0:T(8,128)S(1)}, f32[8,384,128]{2,1,0:T(8,128)S(1)}) custom-call(s32[8,128]{1,0:T(8,128)S(1)} %copy-done.2, bf16[128,1024]{1,0:T(8,128)(2,1)S(1)} %copy-done.1, bf16[1,256,1024]{2,1,0:T(8,128)(2,1)S(1)} %copy-done, ...), custom_call_target="tpu_custom_call", output_to_operand_aliasing={{0}: (5, {})} | custom-call | flops 3221225472 | bytes 1048576 | tf_op jit(solution)/shard_map/slabs3/pallas_call | solution.py:226
  69.3 0.0 collective-permute-done.8.refs_3_
  69.3 2.2 %slabs4.1 = bf16[8,48,1024]{2,1,0:T(8,128)(2,1)S(1)} custom-call(s32[8,128]{1,0:T(8,128)S(1)} %copy-done.2, bf16[128,1024]{1,0:T(8,128)(2,1)S(1)} %copy-done.1, bf16[1,256,1024]{2,1,0:T(8,128)(2,1)S(1)} %copy-done, bf16[2,512,128]{2,1,0:T(8,128)(2,1)S(1)} %collective-permute-done.8.refs_3_, f32[8,384,128]{2,1,0:T(8,128)S(1)} %get-tuple-element.73.refs_4_, ...), custom_call_target="tpu_custom_call" | custom-call | flops 1610612736 | bytes 1048576 | tf_op jit(solution)/shard_map/slabs4/pallas_call | solution.py:226
  71.5 21.0 %all_to_all.5.moved = bf16[8,48,1024]{2,1,0:T(8,128)(2,1)S(1)} all-to-all(bf16[8,48,1024]{2,1,0:T(8,128)(2,1)S(1)} %slabs4.1), channel_id=1, replica_groups=mesh['group'=8,'ctx'=4,'head'=8] {'head'}, dimensions={0} | all-to-all | bytes 1572864 | tf_op jit(solution)/shard_map/all_to_all | solution.py:296
  92.4 1.0 %lay_out.1 = (bf16[16,8192]{1,0:T(8,128)(2,1)}, bf16[1,32,8192]{2,1,0:T(8,128)(2,1)}) custom-call(bf16[8,48,1024]{2,1,0:T(8,128)(2,1)S(1)} %all_to_all.5.moved), custom_call_target="tpu_custom_call" | custom-call | tf_op jit(solution)/shard_map/lay_out/pallas_call | solution.py:252
  (4 shorter events, 0.0 us)
Async XLA Ops:
  0.6 6.1 %collective-permute-start.1 = (bf16[2,128,128]{2,1,0:T(8,128)(2,1)}, bf16[2,128,128]{2,1,0:T(8,128)(2,1)S(1)}, u32[]{:S(2)}, u32[]{:S(2)}) collective-permute-start(bf16[2,128,128]{2,1,0:T(8,128)(2,1)} %param.6), channel_id=1, source_target_pairs={{0,16},{16,0},{8,24},{24,8},{1,17},{17,1},{9,25},{25,9},{2,18},{18... | collective-permute-start | bytes 196616 | tf_op jit(solution)/shard_map/ppermute | solution.py:281
  1.9 4.9 %collective-permute-start = (bf16[2,128,128]{2,1,0:T(8,128)(2,1)}, bf16[2,128,128]{2,1,0:T(8,128)(2,1)S(1)}, u32[]{:S(2)}, u32[]{:S(2)}) collective-permute-start(bf16[2,128,128]{2,1,0:T(8,128)(2,1)} %param.6), channel_id=1, source_target_pairs={{0,8},{8,0},{16,24},{24,16},{1,9},{9,1},{17,25},{25,17},{2,10},{10... | collective-permute-start | bytes 196616 | tf_op jit(solution)/shard_map/ppermute | solution.py:281
  2.9 3.9 %collective-permute-start.2 = (bf16[2,128,128]{2,1,0:T(8,128)(2,1)}, bf16[2,128,128]{2,1,0:T(8,128)(2,1)S(1)}, u32[]{:S(2)}, u32[]{:S(2)}) collective-permute-start(bf16[2,128,128]{2,1,0:T(8,128)(2,1)} %param.6), channel_id=1, source_target_pairs={{0,24},{24,0},{8,16},{16,8},{1,25},{25,1},{9,17},{17,9},{2,26},{26... | collective-permute-start | bytes 196616 | tf_op jit(solution)/shard_map/ppermute | solution.py:281
  3.7 0.8 copy-start.4
  3.7 1.1 %copy-start = (bf16[1,256,1024]{2,1,0:T(8,128)(2,1)S(1)}, bf16[1,256,1024]{2,1,0:T(8,128)(2,1)}, u32[]{:S(2)}) copy-start(bf16[1,256,1024]{2,1,0:T(8,128)(2,1)} %refs_2_.9) | copy-start | bytes 1572868
  3.7 1.1 %copy-start.3 = (bf16[2,1,256,128]{3,2,1,0:T(8,128)(2,1)S(1)}, bf16[2,1,256,128]{3,2,1,0:T(8,128)(2,1)}, u32[]{:S(2)}) copy-start(bf16[2,1,256,128]{3,2,1,0:T(8,128)(2,1)} %kv.1) | copy-start | bytes 393220
  4.5 2.4 %copy-start.1 = (bf16[128,1024]{1,0:T(8,128)(2,1)S(1)}, bf16[128,1024]{1,0:T(8,128)(2,1)}, u32[]{:S(2)}) copy-start(bf16[128,1024]{1,0:T(8,128)(2,1)} %refs_1_.9) | copy-start | bytes 786436
  4.8 0.7 copy-start.2
  6.9 11.8 %collective-permute-start.3 = (bf16[2,512,128]{2,1,0:T(8,128)(2,1)S(1)}, bf16[2,512,128]{2,1,0:T(8,128)(2,1)S(1)}, u32[]{:S(2)}, u32[]{:S(2)}) collective-permute-start(bf16[2,512,128]{2,1,0:T(8,128)(2,1)S(1)} %constant_dynamic-update-slice_fusion.refs_3_), channel_id=1, source_target_pairs={{0,32},{8,232},{16,48},{24,248},{32,64},{40,8},{48,80},{56,24},{64... | collective-permute-start | bytes 786440 | tf_op jit(solution)/shard_map/ppermute | solution.py:275
  18.6 2.3 %collective-permute-start.5 = (bf16[2,512,128]{2,1,0:T(8,128)(2,1)S(1)}, bf16[2,512,128]{2,1,0:T(8,128)(2,1)S(1)}, u32[]{:S(2)}, u32[]{:S(2)}) collective-permute-start(bf16[2,512,128]{2,1,0:T(8,128)(2,1)S(1)} %collective-permute-done.3.refs_3_), channel_id=1, source_target_pairs={{0,8},{8,0},{16,24},{24,16},{1,9},{9,1},{17,25},{25,17},{2,10},{10... | collective-permute-start | bytes 786440 | tf_op jit(solution)/shard_map/ppermute | solution.py:278
  18.7 17.1 %collective-permute-start.4 = (bf16[2,512,128]{2,1,0:T(8,128)(2,1)S(1)}, bf16[2,512,128]{2,1,0:T(8,128)(2,1)S(1)}, u32[]{:S(2)}, u32[]{:S(2)}) collective-permute-start(bf16[2,512,128]{2,1,0:T(8,128)(2,1)S(1)} %collective-permute-done.3.refs_3_), channel_id=1, source_target_pairs={{0,32},{8,232},{16,48},{24,248},{32,64},{40,8},{48,80},{56,24},{64... | collective-permute-start | bytes 786440 | tf_op jit(solution)/shard_map/ppermute | solution.py:275
  35.8 1.8 %collective-permute-start.7 = (bf16[2,512,128]{2,1,0:T(8,128)(2,1)S(1)}, bf16[2,512,128]{2,1,0:T(8,128)(2,1)S(1)}, u32[]{:S(2)}, u32[]{:S(2)}) collective-permute-start(bf16[2,512,128]{2,1,0:T(8,128)(2,1)S(1)} %collective-permute-done.4.refs_3_), channel_id=1, source_target_pairs={{0,8},{8,0},{16,24},{24,16},{1,9},{9,1},{17,25},{25,17},{2,10},{10... | collective-permute-start | bytes 786440 | tf_op jit(solution)/shard_map/ppermute | solution.py:278
  36.1 6.5 %collective-permute-start.6 = (bf16[2,512,128]{2,1,0:T(8,128)(2,1)S(1)}, bf16[2,512,128]{2,1,0:T(8,128)(2,1)S(1)}, u32[]{:S(2)}, u32[]{:S(2)}) collective-permute-start(bf16[2,512,128]{2,1,0:T(8,128)(2,1)S(1)} %collective-permute-done.4.refs_3_), channel_id=1, source_target_pairs={{0,32},{8,232},{16,48},{24,248},{32,64},{40,8},{48,80},{56,24},{64... | collective-permute-start | bytes 786440 | tf_op jit(solution)/shard_map/ppermute | solution.py:275
  42.6 11.5 %collective-permute-start.9 = (bf16[2,512,128]{2,1,0:T(8,128)(2,1)S(1)}, bf16[2,512,128]{2,1,0:T(8,128)(2,1)S(1)}, u32[]{:S(2)}, u32[]{:S(2)}) collective-permute-start(bf16[2,512,128]{2,1,0:T(8,128)(2,1)S(1)} %collective-permute-done.6.refs_3_), channel_id=1, source_target_pairs={{0,8},{8,0},{16,24},{24,16},{1,9},{9,1},{17,25},{25,17},{2,10},{10... | collective-permute-start | bytes 786440 | tf_op jit(solution)/shard_map/ppermute | solution.py:278
  52.8 16.5 %collective-permute-start.8 = (bf16[2,512,128]{2,1,0:T(8,128)(2,1)S(1)}, bf16[2,512,128]{2,1,0:T(8,128)(2,1)S(1)}, u32[]{:S(2)}, u32[]{:S(2)}) collective-permute-start(bf16[2,512,128]{2,1,0:T(8,128)(2,1)S(1)} %collective-permute-done.6.refs_3_), channel_id=1, source_target_pairs={{0,32},{8,232},{16,48},{24,248},{32,64},{40,8},{48,80},{56,24},{64... | collective-permute-start | bytes 786440 | tf_op jit(solution)/shard_map/ppermute | solution.py:275
where the time goes:
time: 95.3 us; the launch traced here: 93.6 us
  Pallas kernels  51.7 us (54%)
  blocking collectives  21 us (22%)
  starting transfers between devices  16.7 us (18%)
  between operations  1.64 us (2%)
  waiting for transfers between devices  1.49 us (2%)
  local copies, waits for them, and re-layouts  1.14 us (1%)
    pallas_call x5, Pallas kernels, attend(): pl.pallas_call(functools.partial(slab_kernel, n, step, last), in_specs=[V...  48.7 us
    all_to_all x1, blocking collectives, body(): lax.all_to_all(mixed, 'head', split_axis=0, concat_axis=0, tiled=True)  21 us
    ppermute x3, starting transfers between devices, swap(): return lax.ppermute(x, 'ctx', C_CORE)  10.5 us
    ppermute x4, starting transfers between devices, pass_on(): return lax.ppermute(x, ('group', 'ctx'), ring)  3.79 us
    ppermute x3, starting transfers between devices, body(): lax.ppermute(prompt_kv, 'ctx', pairs)  2.4 us
  transfers between devices with their start and end apart: 10, of which 1 were waited for; matrix products, arithmetic and copies ran while one was open for 0% of the time, Pallas kernels for 52%

commit v1 on v0

--- a/solution.py
+++ b/solution.py
@@ -102,100 +102,156 @@
             m_out[h, at, :], l_out[h, at, :], acc_out[h, at, :] = weigh(q, kv[0, 0, :n, :], vx[:n, :], *fresh(), mask)
 
 
-def slab_kernel(n_slabs, step, last, *refs):
-    meta, qp, qc = refs[:3]
-    slabs = refs[3 : 3 + n_slabs]
-    m_in, l_in, acc_in = refs[3 + n_slabs : 6 + n_slabs]
-    n_out = 1 if last else 3
-    outs = refs[6 + n_slabs : 6 + n_slabs + n_out]
-    vxs, flag = refs[6 + n_slabs + n_out : -1], refs[-1]
-    for vx, kv in zip(vxs, slabs):
-        extend(vx, kv[1])
-
-    ctx, z = lax.axis_index("ctx"), lax.axis_index("group")
-
-    def own_mask(j, part):
+def sees(step, i):
+    z = lax.axis_index("group")
+    way = 2 * (lax.axis_index("ctx") & 1) - 1
+    return ((z + (1 - 2 * i) * way * step) & 7) < z
+
+
+def read(refs, h, at):
+    return tuple(ref[h, at, :] for ref in refs)
+
+
+def write(refs, h, at, values):
+    for ref, value in zip(refs, values):
+        ref[h, at, :] = value
+
+
+def place(r):
+    return pl.ds(0 if r is None else ROWS_P + r, BLOCK)
+
+
+def queries(qp, qc, h, r):
+    return qp[:, columns(h)] if r is None else qc[0, pl.ds(r, BLOCK), columns(h)]
+
+
+def first_kernel(qp, qc, slab, m_in, l_in, acc_in, m_out, l_out, acc_out, vx):
+    extend(vx, slab[1])
+    ctx = lax.axis_index("ctx")
+
+    def mask(j, part):
         if j == 0:
             row = lax.broadcasted_iota(jnp.int32, (BLOCK, HD), 0)
             col = lax.broadcasted_iota(jnp.int32, (BLOCK, HD), 1)
             return jnp.where(col <= row, part, LOW)
         return jnp.where((ctx ^ j) < ctx, part, LOW)
 
-    def run(h, r, running, over, partly=False):
-        at = pl.ds(0 if r is None else ROWS_P + r, BLOCK)
-        first = step == 0 and r is None
-        state = fresh() if first else tuple(ref[h, at, :] for ref in (m_in, l_in, acc_in))
-        q = qp[:, columns(h)] if r is None else qc[0, pl.ds(r, BLOCK), columns(h)]
-        for i in range(n_slabs) if partly is not None else ():
-            mask = own_mask if first else None
-            if partly:
-                mask = lambda j, part, i=i: jnp.where(sees[i], part, LOW)
-            if running or first:
-                state = weigh(q, slabs[i][0], vxs[i][...], *state, mask)
-            else:
-                *state, over = weigh_kept(q, slabs[i][0], vxs[i][...], *state, over, mask)
-        if not last:
-            if running or first:
-                outs[0][h, at, :] = state[0]
-            outs[1][h, at, :], outs[2][h, at, :] = state[1:]
-            return over
-        mixed = state[2] / state[1]
+    def head(h, carry):
+        for r in (None, 0, BLOCK):
+            state = fresh() if r is None else read((m_in, l_in, acc_in), h, place(r))
+            state = weigh(queries(qp, qc, h, r), slab[0], vx[...], *state, mask if r is None else None)
+            write((m_out, l_out, acc_out), h, place(r), state)
+        return carry
+
+    over_heads(4, head, 0)
+
+
+def rows_kept(blocks, qp, qc, slabs, vxs, m_ref, src, put, seen=None):
+    def head(h, over):
+        for r in blocks:
+            m, l, acc = read((m_ref, *src), h, place(r))
+            for i, slab in enumerate(slabs):
+                mask = None if seen is None else lambda j, part, i=i: jnp.where(seen[i], part, LOW)
+                m, l, acc, over = weigh_kept(queries(qp, qc, h, r), slab[0], vxs[i][...], m, l, acc, over, mask)
+            put(h, r, l, acc)
+        return over
+
+    return over_heads(4, head, jnp.zeros((BLOCK, HD), jnp.float32))
+
+
+def middle_kernel(step, qp, qc, near, other, m_ref, l_in, acc_in, over_in, l_out, acc_out, over_out, *vxs):
+    slabs = (near, other)
+    for vx, kv in zip(vxs, slabs):
+        extend(vx, kv[1])
+    seen = [sees(step, i) for i in range(2)]
+
+    def put(h, r, l, acc):
+        write((l_out, acc_out), h, place(r), (l, acc))
+
+    def rows(blocks, seen=None):
+        over = rows_kept(blocks, qp, qc, slabs, vxs, m_ref, (l_in, acc_in), put, seen)
+        over_out[...] = jnp.maximum(over_out[...], over)
+
+    over_out[...] = jnp.zeros((BLOCK, HD), jnp.float32) if step == 1 else over_in[...]
+    full = seen[0] & seen[1]
+
+    @pl.when(full)
+    def _():
+        rows((None, 0, BLOCK))
+
+    @pl.when(jnp.logical_not(full))
+    def _():
+        rows((0, BLOCK))
+        some = seen[0] | seen[1]
+
+        @pl.when(some)
+        def _():
+            rows((None,), seen)
+
+        if step == 1:
+
+            @pl.when(jnp.logical_not(some))
+            def _():
+                l_out[:, :ROWS_P, :] = l_in[:, :ROWS_P, :]
+                acc_out[:, :ROWS_P, :] = acc_in[:, :ROWS_P, :]
+
+
+def last_kernel(meta, qp, qc, *refs):
+    slabs, far = refs[:7], refs[6]
+    m_ref, l_in, acc_in, over_in, l_first, acc_first, out, vx, flag, *redo = refs[7:]
+    extend(vx, far[1])
+    seen = sees(4, 0)
+
+    def put(h, r, l, acc):
+        mixed = acc / l
         if r is None:
-            outs[0][:, :16, columns(h)] = mixed.reshape(8, 16, HD).astype(jnp.bfloat16)
+            out[:, :16, columns(h)] = mixed.reshape(8, 16, HD).astype(jnp.bfloat16)
         else:
             row = r + lax.broadcasted_iota(jnp.int32, (BLOCK, HD), 0)
             mixed = jnp.where(row < meta[0:1, :], mixed, 0.0).astype(jnp.bfloat16)
-            outs[0][pl.ds(r // 32, BLOCK // 32), 16:, columns(h)] = mixed.reshape(BLOCK // 32, 32, HD)
-        return over
-
-    way = 2 * (ctx & 1) - 1
-    sees = [jnp.bool_(True)] if step == 0 else [((z + (1 - 2 * i) * way * step) & 7) < z for i in range(n_slabs)]
-    none = jnp.zeros((BLOCK, HD), jnp.float32)
-
-    def rows(blocks, running=False, partly=False):
-        def head(h, over):
-            for r in blocks:
-                over = run(h, r, running, over, partly)
-            return over
-
-        return over_heads(1 if running else 4, head, none)
-
-    if step == 0:
-        flag[...] = rows((None, 0, BLOCK))
-    else:
-        full = functools.reduce(jnp.logical_and, sees)
-        some = functools.reduce(jnp.logical_or, sees)
-
-        @pl.when(full)
-        def _():
-            flag[...] = rows((None, 0, BLOCK))
-
-        @pl.when(jnp.logical_not(full))
-        def _():
-            flag[...] = rows((0, BLOCK))
-            if n_slabs > 1:
-
-                @pl.when(some)
-                def _():
-                    flag[...] = jnp.maximum(flag[...], rows((None,), partly=True))
-
-            @pl.when(jnp.logical_not(some))
-            def _():
-                if last:
-                    rows((None,), partly=None)
-                else:
-                    for before, after in ((l_in, outs[1]), (acc_in, outs[2])):
-                        after[:, :ROWS_P, :] = before[:, :ROWS_P, :]
+            out[pl.ds(r // 32, BLOCK // 32), 16:, columns(h)] = mixed.reshape(BLOCK // 32, 32, HD)
+
+    def rows(blocks):
+        over = rows_kept(blocks, qp, qc, (far,), (vx,), m_ref, (l_in, acc_in), put)
+        flag[...] = jnp.maximum(over_in[...], over)
+
+    @pl.when(seen)
+    def _():
+        rows((None, 0, BLOCK))
+
+    @pl.when(jnp.logical_not(seen))
+    def _():
+        rows((0, BLOCK))
+
+        def head(h, carry):
+            put(h, None, l_in[h, place(None), :], acc_in[h, place(None), :])
+            return carry
+
+        over_heads(4, head, 0)
 
     @pl.when(jnp.max(flag[...]) > ROOM)
     def _():
-        rows((0, BLOCK), running=True)
-        rows((None,), running=True, partly=step != 0)
+        for n, slab in enumerate(slabs):
+            extend(vx, slab[1])
+            visible = sees(n // 2 + 1, n % 2)
+
+            def head(h, carry, n=n, slab=slab, visible=visible):
+                for r in (None, 0, BLOCK):
+                    state = read((m_ref, l_first, acc_first) if n == 0 else redo, h, place(r))
+                    mask = (lambda j, part: jnp.where(visible, part, LOW)) if r is None else None
+                    state = weigh(queries(qp, qc, h, r), slab[0], vx[...], *state, mask)
+                    write(redo, h, place(r), state)
+                    if n == 6:
+                        put(h, r, *state[1:])
+                return carry
+
+            over_heads(1, head, 0)
 
 
 VMEM = pl.BlockSpec(memory_space=pltpu.VMEM)
 ANY = pl.BlockSpec(memory_space=pl.ANY)
 STATE = (jax.ShapeDtypeStruct((GQA, ROWS, HD), jnp.float32),) * 3
+EXCESS = jax.ShapeDtypeStruct((BLOCK, HD), jnp.float32)
 PARAMS = pltpu.CompilerParams(vmem_limit_bytes=32 << 20)
 
 
@@ -203,37 +259,37 @@
     return pl.CostEstimate(flops=scores * 512 * 2, bytes_accessed=1 << 20, transcendentals=scores)
 
 
-def attend_own(meta, qc, kv):
+def call(kernel, name, scores, n_in, out_shape, alias, scratch, more=()):
     return pl.pallas_call(
-        own_kernel,
-        in_specs=[VMEM] * 3,
-        out_specs=(VMEM,) * 3,
-        out_shape=STATE,
-        scratch_shapes=[pltpu.VMEM((ROWS_C, 2 * HD), jnp.bfloat16)],
-        compiler_params=PARAMS,
-        cost_estimate=cost(GQA * ROWS_C * ROWS_C),
-        name="own",
-    )(meta, qc, kv)
-
-
-def attend(meta, qp, qc, slabs, state, step, last=False):
-    n = len(slabs)
-    if last:
-        out_specs, alias = VMEM, {}
-        out_shape = jax.ShapeDtypeStruct((8, 48, GQA * HD), jnp.bfloat16)
-    else:
-        out_specs, out_shape, alias = (VMEM,) * 3, STATE, {3 + n: 0}
-    return pl.pallas_call(
-        functools.partial(slab_kernel, n, step, last),
-        in_specs=[VMEM] * (n + 6),
-        out_specs=out_specs,
+        kernel,
+        in_specs=[VMEM] * n_in,
+        out_specs=jax.tree.map(lambda _: VMEM, out_shape),
         out_shape=out_shape,
         input_output_aliases=alias,
-        scratch_shapes=[pltpu.VMEM((SLAB, 2 * HD), jnp.bfloat16)] * n + [pltpu.VMEM((BLOCK, HD), jnp.float32)],
+        scratch_shapes=[pltpu.VMEM((n, 2 * HD), jnp.bfloat16) for n in scratch] + [pltpu.VMEM(x.shape, x.dtype) for x in more],
         compiler_params=PARAMS,
-        cost_estimate=cost(GQA * ROWS * SLAB * n),
-        name=f"slabs{step}",
-    )(meta, qp, qc, *slabs, *state)
+        cost_estimate=cost(scores),
+        name=name,
+    )
+
+
+def attend_own(*args):
+    return call(own_kernel, "own", GQA * ROWS_C * ROWS_C, 3, STATE, {}, [ROWS_C])(*args)
+
+
+def attend_first(*args):
+    return call(first_kernel, "first", GQA * ROWS * SLAB, 6, STATE, {3: 0, 4: 1, 5: 2}, [SLAB])(*args)
+
+
+def attend_middle(step, *args):
+    alias = {} if step == 1 else {5: 0, 6: 1, 7: 2}
+    kernel = functools.partial(middle_kernel, step)
+    return call(kernel, f"middle{step}", GQA * ROWS * SLAB * 2, 8, (*STATE[1:], EXCESS), alias, [SLAB] * 2)(*args)
+
+
+def attend_last(*args):
+    out = jax.ShapeDtypeStruct((8, 48, GQA * HD), jnp.bfloat16)
+    return call(last_kernel, "last", GQA * ROWS * SLAB, 16, out, {}, [SLAB], (EXCESS, *STATE))(*args)
 
 
 def lay_out_kernel(moved, prompt_out, cont_out, sems):
@@ -284,15 +340,18 @@
     own = jnp.concatenate([prompt_kv] + pieces, axis=1)
 
     near = pass_on(own)
-    state = attend(meta, prompt_q, cont_q, [own], state, 0)
-    near, state = tie(near, state)
-
+    m, l, acc = attend_first(prompt_q, cont_q, own, *state)
+    near, m, l, acc = tie(near, m, l, acc)
+    l_first, acc_first = l, acc
+
+    over, slabs = jnp.zeros(EXCESS.shape, EXCESS.dtype), []
     for step in (1, 2, 3):
         other = swap(near)
+        slabs += [near, other]
         coming = pass_on(near)
-        state = attend(meta, prompt_q, cont_q, [near, other], state, step)
-        near, state = tie(coming, state)
-    mixed = attend(meta, prompt_q, cont_q, [near], state, 4, last=True)
+        l, acc, over = attend_middle(step, prompt_q, cont_q, near, other, m, l, acc, over)
+        near, l, acc, over = tie(coming, l, acc, over)
+    mixed = attend_last(meta, prompt_q, cont_q, *slabs, near, m, l, acc, over, l_first, acc_first)
     moved = lax.all_to_all(mixed, "head", split_axis=0, concat_axis=0, tiled=True)
     return lay_out(moved)
 

time: 95.3 us -> 97.1 us (1.019)
  the two profiles are of different devices: /device:TPU:97 before, /device:TPU:2 now
where the time goes in v1:
time: 97.1 us; the launch traced here: 96.9 us
  Pallas kernels  52.6 us (54%)
  waiting for transfers between devices  19.2 us (20%)
  blocking collectives  18.9 us (19%)
  starting transfers between devices  3.53 us (4%)
  between operations  1.58 us (2%)
  local copies, waits for them, and re-layouts  1.15 us (1%)
    pallas_call x1, Pallas kernels, attend_last(): call(last_kernel, 'last', GQA * ROWS * SLAB, 16, out, {}, [SLAB], (EXCESS...  37.4 us
    all_to_all x1, blocking collectives, body(): lax.all_to_all(mixed, 'head', split_axis=0, concat_axis=0, tiled=True)  18.9 us
    ppermute x4, waiting for transfers between devices, pass_on(): return lax.ppermute(x, ('group', 'ctx'), ring)  14.1 us
    pallas_call x3, Pallas kernels, attend_middle(): call(kernel, f'middle{step}', GQA * ROWS * SLAB * 2, 8, (*STATE[1:], EXCE...  9.27 us
    ppermute x3, waiting for transfers between devices, swap(): return lax.ppermute(x, 'ctx', C_CORE)  4.59 us
    pallas_call x1, Pallas kernels, attend_first(): call(first_kernel, 'first', GQA * ROWS * SLAB, 6, STATE, {3: 0, 4: 1, 5:...  2.99 us
    ppermute x3, starting transfers between devices, body(): lax.ppermute(prompt_kv, 'ctx', pairs)  2.5 us
  transfers between devices with their start and end apart: 10, of which 8 were waited for; matrix products, arithmetic and copies ran while one was open for 0% of the time, Pallas kernels for 15%

profile of v1, /device:TPU:2, one launch (start us, length us, event | category | flops | bytes accessed | tf_op | source)
XLA Modules:
  0.0 96.9 jit_solution(9731755200531502344)
XLA Ops:
  0.6 0.1 collective-permute-start
  0.7 2.4 %collective-permute-start.1 = (bf16[2,128,128]{2,1,0:T(8,128)(2,1)}, bf16[2,128,128]{2,1,0:T(8,128)(2,1)S(1)}, u32[]{:S(2)}, u32[]{:S(2)}) collective-permute-start(bf16[2,128,128]{2,1,0:T(8,128)(2,1)} %param.6), channel_id=1, source_target_pairs={{0,16},{16,0},{8,24},{24,8},{1,17},{17,1},{9,25},{25,9},{2,18},{18... | collective-permute-start | bytes 196616 | tf_op jit(solution)/shard_map/ppermute | solution.py:337
  3.1 0.1 collective-permute-start.2
  3.8 0.0 copy-start.4
  3.8 0.0 copy-start
  3.8 0.0 copy-start.3
  3.8 0.7 spread.1.meta
  4.5 0.1 copy-done.4
  4.6 0.0 copy-start.1
  4.6 0.2 copy-done
  4.9 0.0 copy-done.3
  4.9 0.0 copy-start.2
  4.9 0.7 copy-done.2
  5.6 1.3 %own.1 = (f32[8,384,128]{2,1,0:T(8,128)S(1)}, f32[8,384,128]{2,1,0:T(8,128)S(1)}, f32[8,384,128]{2,1,0:T(8,128)S(1)}) custom-call(s32[8,128]{1,0:T(8,128)S(1)} %copy-done.2, bf16[1,256,1024]{2,1,0:T(8,128)(2,1)S(1)} %copy-done, bf16[2,1,256,128]{3,2,1,0:T(8,128)(2,1)S(1)} %copy-done.3), custom_call_target="tpu_custom_call" | custom-call | flops 536870912 | bytes 1048576 | tf_op jit(solution)/shard_map/own/pallas_call | solution.py:277
  6.9 0.0 collective-permute-done
  6.9 0.0 collective-permute-done.1
  6.9 0.5 collective-permute-done.2
  7.4 1.0 %collective-permute-start.3 = (bf16[2,512,128]{2,1,0:T(8,128)(2,1)S(1)}, bf16[2,512,128]{2,1,0:T(8,128)(2,1)S(1)}, u32[]{:S(2)}, u32[]{:S(2)}) collective-permute-start(bf16[2,512,128]{2,1,0:T(8,128)(2,1)S(1)} %constant_dynamic-update-slice_fusion.slab), channel_id=1, source_target_pairs={{0,32},{8,232},{16,48},{24,248},{32,64},{40,8},{48,80},{56,24},{64... | collective-permute-start | bytes 786440 | tf_op jit(solution)/shard_map/ppermute | solution.py:331
  8.4 0.0 copy-done.1
  8.4 3.0 %first.1 = (f32[8,384,128]{2,1,0:T(8,128)S(1)}, f32[8,384,128]{2,1,0:T(8,128)S(1)}, f32[8,384,128]{2,1,0:T(8,128)S(1)}) custom-call(bf16[128,1024]{1,0:T(8,128)(2,1)S(1)} %copy-done.1, bf16[1,256,1024]{2,1,0:T(8,128)(2,1)S(1)} %copy-done, ...), custom_call_target="tpu_custom_call", output_to_operand_aliasing={{0}: (3, {}), {1}: (4, {}), {2}: (5, {})} | custom-call | flops 1610612736 | bytes 1048576 | tf_op jit(solution)/shard_map/first/pallas_call | solution.py:281
  11.4 5.3 %collective-permute-done.3.near.refs_0_ = bf16[2,512,128]{2,1,0:T(8,128)(2,1)S(1)} collective-permute-done((bf16[2,512,128]{2,1,0:T(8,128)(2,1)S(1)}, bf16[2,512,128]{2,1,0:T(8,128)(2,1)S(1)}, u32[]{:S(2)}, u32[]{:S(2)}) %collective-permute-start.3) | collective-permute-done | bytes 262176 | tf_op jit(solution)/shard_map/ppermute | solution.py:331
  16.7 0.0 collective-permute-start.4
  16.7 0.0 collective-permute-start.5
  16.7 1.5 %collective-permute-done.4.other.refs_1_ = bf16[2,512,128]{2,1,0:T(8,128)(2,1)S(1)} collective-permute-done((bf16[2,512,128]{2,1,0:T(8,128)(2,1)S(1)}, bf16[2,512,128]{2,1,0:T(8,128)(2,1)S(1)}, u32[]{:S(2)}, u32[]{:S(2)}) %collective-permute-start.4) | collective-permute-done | bytes 262176 | tf_op jit(solution)/shard_map/ppermute | solution.py:334
  18.3 3.0 %middle1.1 = (f32[8,384,128]{2,1,0:T(8,128)S(1)}, f32[8,384,128]{2,1,0:T(8,128)S(1)}, f32[128,128]{1,0:T(8,128)S(1)}) custom-call(bf16[128,1024]{1,0:T(8,128)(2,1)S(1)} %copy-done.1, bf16[1,256,1024]{2,1,0:T(8,128)(2,1)S(1)} %copy-done, bf16[2,512,128]{2,1,0:T(8,128)(2,1)S(1)} %collective-permute-done.3.near.refs_0_, ...), custom_call_target="tpu_custom_call" | custom-call | flops 3221225472 | bytes 1048576 | tf_op jit(solution)/shard_map/middle1/pallas_call | solution.py:287
  21.3 3.0 %collective-permute-done.5.near.refs_2_ = bf16[2,512,128]{2,1,0:T(8,128)(2,1)S(1)} collective-permute-done((bf16[2,512,128]{2,1,0:T(8,128)(2,1)S(1)}, bf16[2,512,128]{2,1,0:T(8,128)(2,1)S(1)}, u32[]{:S(2)}, u32[]{:S(2)}) %collective-permute-start.5) | collective-permute-done | bytes 262176 | tf_op jit(solution)/shard_map/ppermute | solution.py:331
  24.3 0.0 collective-permute-start.6
  24.3 0.0 collective-permute-start.7
  24.3 1.5 %collective-permute-done.6.other.refs_3_ = bf16[2,512,128]{2,1,0:T(8,128)(2,1)S(1)} collective-permute-done((bf16[2,512,128]{2,1,0:T(8,128)(2,1)S(1)}, bf16[2,512,128]{2,1,0:T(8,128)(2,1)S(1)}, u32[]{:S(2)}, u32[]{:S(2)}) %collective-permute-start.6) | collective-permute-done | bytes 262176 | tf_op jit(solution)/shard_map/ppermute | solution.py:334
  25.8 3.2 %middle2.1 = (f32[8,384,128]{2,1,0:T(8,128)S(1)}, f32[8,384,128]{2,1,0:T(8,128)S(1)}, f32[128,128]{1,0:T(8,128)S(1)}) custom-call(bf16[128,1024]{1,0:T(8,128)(2,1)S(1)} %copy-done.1, bf16[1,256,1024]{2,1,0:T(8,128)(2,1)S(1)} %copy-done, ...), custom_call_target="tpu_custom_call", output_to_operand_aliasing={{0}: (5, {}), {1}: (6, {}), {2}: (7, {})} | custom-call | flops 3221225472 | bytes 1048576 | tf_op jit(solution)/shard_map/middle2/pallas_call | solution.py:287
  29.1 2.8 %collective-permute-done.7.near.refs_4_ = bf16[2,512,128]{2,1,0:T(8,128)(2,1)S(1)} collective-permute-done((bf16[2,512,128]{2,1,0:T(8,128)(2,1)S(1)}, bf16[2,512,128]{2,1,0:T(8,128)(2,1)S(1)}, u32[]{:S(2)}, u32[]{:S(2)}) %collective-permute-start.7) | collective-permute-done | bytes 262176 | tf_op jit(solution)/shard_map/ppermute | solution.py:331
  31.9 0.0 collective-permute-start.8
  31.9 0.0 collective-permute-start.9
  31.9 1.5 %collective-permute-done.8.other.refs_5_ = bf16[2,512,128]{2,1,0:T(8,128)(2,1)S(1)} collective-permute-done((bf16[2,512,128]{2,1,0:T(8,128)(2,1)S(1)}, bf16[2,512,128]{2,1,0:T(8,128)(2,1)S(1)}, u32[]{:S(2)}, u32[]{:S(2)}) %collective-permute-start.8) | collective-permute-done | bytes 262176 | tf_op jit(solution)/shard_map/ppermute | solution.py:334
  33.4 3.0 %middle3.1 = (f32[8,384,128]{2,1,0:T(8,128)S(1)}, f32[8,384,128]{2,1,0:T(8,128)S(1)}, f32[128,128]{1,0:T(8,128)S(1)}) custom-call(bf16[128,1024]{1,0:T(8,128)(2,1)S(1)} %copy-done.1, bf16[1,256,1024]{2,1,0:T(8,128)(2,1)S(1)} %copy-done, ...), custom_call_target="tpu_custom_call", output_to_operand_aliasing={{0}: (5, {}), {1}: (6, {}), {2}: (7, {})} | custom-call | flops 3221225472 | bytes 1048576 | tf_op jit(solution)/shard_map/middle3/pallas_call | solution.py:287
  36.5 3.0 %collective-permute-done.9.refs_6_ = bf16[2,512,128]{2,1,0:T(8,128)(2,1)S(1)} collective-permute-done((bf16[2,512,128]{2,1,0:T(8,128)(2,1)S(1)}, bf16[2,512,128]{2,1,0:T(8,128)(2,1)S(1)}, u32[]{:S(2)}, u32[]{:S(2)}) %collective-permute-start.9) | collective-permute-done | bytes 262176 | tf_op jit(solution)/shard_map/ppermute | solution.py:331
  39.5 37.4 %last.1 = bf16[8,48,1024]{2,1,0:T(8,128)(2,1)S(1)} custom-call(s32[8,128]{1,0:T(8,128)S(1)} %copy-done.2, bf16[128,1024]{1,0:T(8,128)(2,1)S(1)} %copy-done.1, bf16[1,256,1024]{2,1,0:T(8,128)(2,1)S(1)} %copy-done, bf16[2,512,128]{2,1,0:T(8,128)(2,1)S(1)} %collective-permute-done.3.near.refs_0_, bf16[2,512,128]{2,1,0:T(8,128)(2,1)S(1)} %collective-permute-done.4.other.refs_1_, ...), custom_call_target="tpu_custom_call" | custom-call | flops 1610612736 | bytes 1048576 | tf_op jit(solution)/shard_map/last/pallas_call | solution.py:292
  76.9 18.9 %all_to_all.5.moved = bf16[8,48,1024]{2,1,0:T(8,128)(2,1)S(1)} all-to-all(bf16[8,48,1024]{2,1,0:T(8,128)(2,1)S(1)} %last.1), channel_id=1, replica_groups=mesh['group'=8,'ctx'=4,'head'=8] {'head'}, dimensions={0} | all-to-all | bytes 1572864 | tf_op jit(solution)/shard_map/all_to_all | solution.py:355
  95.7 1.0 %lay_out.1 = (bf16[16,8192]{1,0:T(8,128)(2,1)}, bf16[1,32,8192]{2,1,0:T(8,128)(2,1)}) custom-call(bf16[8,48,1024]{2,1,0:T(8,128)(2,1)S(1)} %all_to_all.5.moved), custom_call_target="tpu_custom_call" | custom-call | tf_op jit(solution)/shard_map/lay_out/pallas_call | solution.py:308
  (5 shorter events, 0.1 us)
Async XLA Ops:
  0.6 6.3 %collective-permute-start = (bf16[2,128,128]{2,1,0:T(8,128)(2,1)}, bf16[2,128,128]{2,1,0:T(8,128)(2,1)S(1)}, u32[]{:S(2)}, u32[]{:S(2)}) collective-permute-start(bf16[2,128,128]{2,1,0:T(8,128)(2,1)} %param.6), channel_id=1, source_target_pairs={{0,8},{8,0},{16,24},{24,16},{1,9},{9,1},{17,25},{25,17},{2,10},{10... | collective-permute-start | bytes 196616 | tf_op jit(solution)/shard_map/ppermute | solution.py:337
  0.7 6.2 %collective-permute-start.1 = (bf16[2,128,128]{2,1,0:T(8,128)(2,1)}, bf16[2,128,128]{2,1,0:T(8,128)(2,1)S(1)}, u32[]{:S(2)}, u32[]{:S(2)}) collective-permute-start(bf16[2,128,128]{2,1,0:T(8,128)(2,1)} %param.6), channel_id=1, source_target_pairs={{0,16},{16,0},{8,24},{24,8},{1,17},{17,1},{9,25},{25,9},{2,18},{18... | collective-permute-start | bytes 196616 | tf_op jit(solution)/shard_map/ppermute | solution.py:337
  3.1 4.3 %collective-permute-start.2 = (bf16[2,128,128]{2,1,0:T(8,128)(2,1)}, bf16[2,128,128]{2,1,0:T(8,128)(2,1)S(1)}, u32[]{:S(2)}, u32[]{:S(2)}) collective-permute-start(bf16[2,128,128]{2,1,0:T(8,128)(2,1)} %param.6), channel_id=1, source_target_pairs={{0,24},{24,0},{8,16},{16,8},{1,25},{25,1},{9,17},{17,9},{2,26},{26... | collective-permute-start | bytes 196616 | tf_op jit(solution)/shard_map/ppermute | solution.py:337
  3.8 0.8 copy-start.4
  3.8 1.1 %copy-start = (bf16[1,256,1024]{2,1,0:T(8,128)(2,1)S(1)}, bf16[1,256,1024]{2,1,0:T(8,128)(2,1)}, u32[]{:S(2)}) copy-start(bf16[1,256,1024]{2,1,0:T(8,128)(2,1)} %qc.11) | copy-start | bytes 1572868
  3.8 1.1 %copy-start.3 = (bf16[2,1,256,128]{3,2,1,0:T(8,128)(2,1)S(1)}, bf16[2,1,256,128]{3,2,1,0:T(8,128)(2,1)}, u32[]{:S(2)}) copy-start(bf16[2,1,256,128]{3,2,1,0:T(8,128)(2,1)} %kv.1) | copy-start | bytes 393220
  4.6 3.8 %copy-start.1 = (bf16[128,1024]{1,0:T(8,128)(2,1)S(1)}, bf16[128,1024]{1,0:T(8,128)(2,1)}, u32[]{:S(2)}) copy-start(bf16[128,1024]{1,0:T(8,128)(2,1)} %qp.9) | copy-start | bytes 786436
  4.9 0.7 copy-start.2
  7.4 9.3 %collective-permute-start.3 = (bf16[2,512,128]{2,1,0:T(8,128)(2,1)S(1)}, bf16[2,512,128]{2,1,0:T(8,128)(2,1)S(1)}, u32[]{:S(2)}, u32[]{:S(2)}) collective-permute-start(bf16[2,512,128]{2,1,0:T(8,128)(2,1)S(1)} %constant_dynamic-update-slice_fusion.slab), channel_id=1, source_target_pairs={{0,32},{8,232},{16,48},{24,248},{32,64},{40,8},{48,80},{56,24},{64... | collective-permute-start | bytes 786440 | tf_op jit(solution)/shard_map/ppermute | solution.py:331
  16.7 1.5 %collective-permute-start.4 = (bf16[2,512,128]{2,1,0:T(8,128)(2,1)S(1)}, bf16[2,512,128]{2,1,0:T(8,128)(2,1)S(1)}, u32[]{:S(2)}, u32[]{:S(2)}) collective-permute-start(bf16[2,512,128]{2,1,0:T(8,128)(2,1)S(1)} %collective-permute-done.3.near.refs_0_), channel_id=1, source_target_pairs={{0,8},{8,0},{16,24},{24,16},{1,9},{9,1},{17,25},{25,17},{2,10},{10... | collective-permute-start | bytes 786440 | tf_op jit(solution)/shard_map/ppermute | solution.py:334
  16.7 7.6 %collective-permute-start.5 = (bf16[2,512,128]{2,1,0:T(8,128)(2,1)S(1)}, bf16[2,512,128]{2,1,0:T(8,128)(2,1)S(1)}, u32[]{:S(2)}, u32[]{:S(2)}) collective-permute-start(bf16[2,512,128]{2,1,0:T(8,128)(2,1)S(1)} %collective-permute-done.3.near.refs_0_), channel_id=1, source_target_pairs={{0,32},{8,232},{16,48},{24,248},{32,64},{40,8},{48,80},{56,24},{64... | collective-permute-start | bytes 786440 | tf_op jit(solution)/shard_map/ppermute | solution.py:331
  24.3 1.5 %collective-permute-start.6 = (bf16[2,512,128]{2,1,0:T(8,128)(2,1)S(1)}, bf16[2,512,128]{2,1,0:T(8,128)(2,1)S(1)}, u32[]{:S(2)}, u32[]{:S(2)}) collective-permute-start(bf16[2,512,128]{2,1,0:T(8,128)(2,1)S(1)} %collective-permute-done.5.near.refs_2_), channel_id=1, source_target_pairs={{0,8},{8,0},{16,24},{24,16},{1,9},{9,1},{17,25},{25,17},{2,10},{10... | collective-permute-start | bytes 786440 | tf_op jit(solution)/shard_map/ppermute | solution.py:334
  24.3 7.6 %collective-permute-start.7 = (bf16[2,512,128]{2,1,0:T(8,128)(2,1)S(1)}, bf16[2,512,128]{2,1,0:T(8,128)(2,1)S(1)}, u32[]{:S(2)}, u32[]{:S(2)}) collective-permute-start(bf16[2,512,128]{2,1,0:T(8,128)(2,1)S(1)} %collective-permute-done.5.near.refs_2_), channel_id=1, source_target_pairs={{0,32},{8,232},{16,48},{24,248},{32,64},{40,8},{48,80},{56,24},{64... | collective-permute-start | bytes 786440 | tf_op jit(solution)/shard_map/ppermute | solution.py:331
  31.9 1.5 %collective-permute-start.8 = (bf16[2,512,128]{2,1,0:T(8,128)(2,1)S(1)}, bf16[2,512,128]{2,1,0:T(8,128)(2,1)S(1)}, u32[]{:S(2)}, u32[]{:S(2)}) collective-permute-start(bf16[2,512,128]{2,1,0:T(8,128)(2,1)S(1)} %collective-permute-done.7.near.refs_4_), channel_id=1, source_target_pairs={{0,8},{8,0},{16,24},{24,16},{1,9},{9,1},{17,25},{25,17},{2,10},{10... | collective-permute-start | bytes 786440 | tf_op jit(solution)/shard_map/ppermute | solution.py:334
  31.9 7.6 %collective-permute-start.9 = (bf16[2,512,128]{2,1,0:T(8,128)(2,1)S(1)}, bf16[2,512,128]{2,1,0:T(8,128)(2,1)S(1)}, u32[]{:S(2)}, u32[]{:S(2)}) collective-permute-start(bf16[2,512,128]{2,1,0:T(8,128)(2,1)S(1)} %collective-permute-done.7.near.refs_4_), channel_id=1, source_target_pairs={{0,32},{8,232},{16,48},{24,248},{32,64},{40,8},{48,80},{56,24},{64... | collective-permute-start | bytes 786440 | tf_op jit(solution)/shard_map/ppermute | solution.py:331

commit v2 on v1

--- a/solution.py
+++ b/solution.py
@@ -334,14 +334,18 @@
         return lax.ppermute(x, "ctx", C_CORE)
 
     meta = spread(cont_len)
-    pieces = [lax.ppermute(prompt_kv, "ctx", pairs) for pairs in (C_CORE, C_X, C_DIAG)]
+    partner, across, diagonal = (lax.ppermute(prompt_kv, "ctx", pairs) for pairs in (C_CORE, C_X, C_DIAG))
+    chip = jnp.concatenate([prompt_kv, partner], axis=1)
+    chip, meta = tie(chip, meta)
+    near_chip = pass_on(chip)
     state = attend_own(meta, cont_q, cont_kv)
-    pieces, state = tie(pieces, state)
-    own = jnp.concatenate([prompt_kv] + pieces, axis=1)
-
-    near = pass_on(own)
+    across, diagonal, state = tie(across, diagonal, state)
+    other_chip = jnp.concatenate([across, diagonal], axis=1)
+    near_other = pass_on(other_chip)
+    own = jnp.concatenate([chip, other_chip], axis=1)
     m, l, acc = attend_first(prompt_q, cont_q, own, *state)
-    near, m, l, acc = tie(near, m, l, acc)
+    near_chip, near_other, m, l, acc = tie(near_chip, near_other, m, l, acc)
+    near = jnp.concatenate([near_chip, near_other], axis=1)
     l_first, acc_first = l, acc
 
     over, slabs = jnp.zeros(EXCESS.shape, EXCESS.dtype), []

time: 97.1 us -> 97.3 us (level)
  starting transfers between devices: 3.53 us -> 6.01 us
  waiting for transfers between devices: 19.2 us -> 17.1 us
    ppermute x4 -> x5, starting transfers between devices: 1.02 us -> 3.41 us  [pass_on(): return lax.ppermute(x, ('group', 'ctx'), ring)]
    ppermute x4 -> x5, waiting for transfers between devices: 14.1 us -> 12.5 us  [pass_on(): return lax.ppermute(x, ('group', 'ctx'), ring)]
  transfers between devices with their start and end apart: 10 -> 11, of which waited for: 8 -> 8; matrix products, arithmetic and copies ran while one was open for 0% -> 0% of each run, Pallas kernels for 15% -> 14%
where the time goes in v2:
time: 97.3 us; the launch traced here: 97.1 us
  Pallas kernels  52.4 us (54%)
  blocking collectives  18.9 us (19%)
  waiting for transfers between devices  17.1 us (18%)
  starting transfers between devices  6.01 us (6%)
  between operations  1.6 us (2%)
  local copies, waits for them, and re-layouts  1.12 us (1%)
    pallas_call x1, Pallas kernels, attend_last(): call(last_kernel, 'last', GQA * ROWS * SLAB, 16, out, {}, [SLAB], (EXCESS...  37.4 us
    all_to_all x1, blocking collectives, body(): lax.all_to_all(mixed, 'head', split_axis=0, concat_axis=0, tiled=True)  18.9 us
    ppermute x5, waiting for transfers between devices, pass_on(): return lax.ppermute(x, ('group', 'ctx'), ring)  12.5 us
    pallas_call x3, Pallas kernels, attend_middle(): call(kernel, f'middle{step}', GQA * ROWS * SLAB * 2, 8, (*STATE[1:], EXCE...  9.09 us
    ppermute x3, waiting for transfers between devices, swap(): return lax.ppermute(x, 'ctx', C_CORE)  4.11 us
    ppermute x5, starting transfers between devices, pass_on(): return lax.ppermute(x, ('group', 'ctx'), ring)  3.41 us
    pallas_call x1, Pallas kernels, attend_first(): call(first_kernel, 'first', GQA * ROWS * SLAB, 6, STATE, {3: 0, 4: 1, 5:...  2.99 us
    ppermute x3, starting transfers between devices, body(): lax.ppermute(prompt_kv, 'ctx', pairs)  2.5 us
  transfers between devices with their start and end apart: 11, of which 8 were waited for; matrix products, arithmetic and copies ran while one was open for 0% of the time, Pallas kernels for 14%

profile of v2, /device:TPU:2, one launch (start us, length us, event | category | flops | bytes accessed | tf_op | source)
XLA Modules:
  0.0 97.1 jit_solution(14304226756809612761)
XLA Ops:
  0.6 0.1 collective-permute-start
  0.7 2.4 %collective-permute-start.2 = (bf16[2,128,128]{2,1,0:T(8,128)(2,1)}, bf16[2,128,128]{2,1,0:T(8,128)(2,1)S(1)}, u32[]{:S(2)}, u32[]{:S(2)}) collective-permute-start(bf16[2,128,128]{2,1,0:T(8,128)(2,1)} %param.6), channel_id=1, source_target_pairs={{0,16},{16,0},{8,24},{24,8},{1,17},{17,1},{9,25},{25,9},{2,18},{18... | collective-permute-start | bytes 196616 | tf_op jit(solution)/shard_map/ppermute | solution.py:337
  3.1 0.1 collective-permute-start.3
  3.8 0.0 copy-start.4
  3.8 0.0 copy-start
  3.8 0.0 copy-start.3
  3.8 0.7 spread.1.meta
  4.5 0.0 copy-start.1
  4.5 0.0 collective-permute-done
  4.5 0.1 copy-done.4
  4.6 0.2 copy-done
  4.9 0.0 copy-done.3
  4.9 0.0 copy-start.2
  4.9 0.7 copy-done.2
  5.6 1.3 %own.1 = (f32[8,384,128]{2,1,0:T(8,128)S(1)}, f32[8,384,128]{2,1,0:T(8,128)S(1)}, f32[8,384,128]{2,1,0:T(8,128)S(1)}) custom-call(s32[8,128]{1,0:T(8,128)S(1)} %copy-done.2, bf16[1,256,1024]{2,1,0:T(8,128)(2,1)S(1)} %copy-done, bf16[2,1,256,128]{3,2,1,0:T(8,128)(2,1)S(1)} %copy-done.3), custom_call_target="tpu_custom_call" | custom-call | flops 536870912 | bytes 1048576 | tf_op jit(solution)/shard_map/own/pallas_call | solution.py:277
  6.9 0.0 collective-permute-done.2
  6.9 0.5 collective-permute-done.3
  7.4 1.0 %collective-permute-start.1 = (bf16[2,256,128]{2,1,0:T(8,128)(2,1)S(1)}, bf16[2,256,128]{2,1,0:T(8,128)(2,1)S(1)}, u32[]{:S(2)}, u32[]{:S(2)}) collective-permute-start(bf16[2,256,128]{2,1,0:T(8,128)(2,1)S(1)} %pad_maximum_fusion.1), channel_id=1, source_target_pairs={{0,32},{8,232},{16,48},{24,248},{32,64},{40,8},{48,80},{56,24},{64... | collective-permute-start | bytes 393224 | tf_op jit(solution)/shard_map/ppermute | solution.py:331
  8.4 1.9 %collective-permute-start.4 = (bf16[2,256,128]{2,1,0:T(8,128)(2,1)S(1)}, bf16[2,256,128]{2,1,0:T(8,128)(2,1)S(1)}, u32[]{:S(2)}, u32[]{:S(2)}) collective-permute-start(bf16[2,256,128]{2,1,0:T(8,128)(2,1)S(1)} %pad_maximum_fusion.2), channel_id=1, source_target_pairs={{0,32},{8,232},{16,48},{24,248},{32,64},{40,8},{48,80},{56,24},{64... | collective-permute-start | bytes 393224 | tf_op jit(solution)/shard_map/ppermute | solution.py:331
  10.3 0.0 copy-done.1
  10.3 3.0 %first.1 = (f32[8,384,128]{2,1,0:T(8,128)S(1)}, f32[8,384,128]{2,1,0:T(8,128)S(1)}, f32[8,384,128]{2,1,0:T(8,128)S(1)}) custom-call(bf16[128,1024]{1,0:T(8,128)(2,1)S(1)} %copy-done.1, bf16[1,256,1024]{2,1,0:T(8,128)(2,1)S(1)} %copy-done, bf16[2,512,128]{2,1,0:T(8,128)(2,1)S(1)} %pad_maximum_fusion.slab, ...), custom_call_target="tpu_custom_call", output_to_operand_aliasing={{0}: (3, {}), {1}: (4, {}), {2}: (5, {})} | custom-call | flops 1610612736 | bytes 1048576 | tf_op jit(solution)/shard_map/first/pallas_call | solution.py:281
  13.3 3.4 %collective-permute-done.4 = bf16[2,256,128]{2,1,0:T(8,128)(2,1)S(1)} collective-permute-done((bf16[2,256,128]{2,1,0:T(8,128)(2,1)S(1)}, bf16[2,256,128]{2,1,0:T(8,128)(2,1)S(1)}, u32[]{:S(2)}, u32[]{:S(2)}) %collective-permute-start.4) | collective-permute-done | bytes 131104 | tf_op jit(solution)/shard_map/ppermute | solution.py:331
  16.7 0.0 collective-permute-done.1
  16.8 0.1 collective-permute-start.5
  16.9 0.5 collective-permute-start.6
  17.3 1.1 %collective-permute-done.5.other.refs_1_ = bf16[2,512,128]{2,1,0:T(8,128)(2,1)S(1)} collective-permute-done((bf16[2,512,128]{2,1,0:T(8,128)(2,1)S(1)}, bf16[2,512,128]{2,1,0:T(8,128)(2,1)S(1)}, u32[]{:S(2)}, u32[]{:S(2)}) %collective-permute-start.5) | collective-permute-done | bytes 262176 | tf_op jit(solution)/shard_map/ppermute | solution.py:334
  18.4 3.0 %middle1.1 = (f32[8,384,128]{2,1,0:T(8,128)S(1)}, f32[8,384,128]{2,1,0:T(8,128)S(1)}, f32[128,128]{1,0:T(8,128)S(1)}) custom-call(bf16[128,1024]{1,0:T(8,128)(2,1)S(1)} %copy-done.1, bf16[1,256,1024]{2,1,0:T(8,128)(2,1)S(1)} %copy-done, bf16[2,512,128]{2,1,0:T(8,128)(2,1)S(1)} %constant_dynamic-update-slice_fusion.near.refs_0_, ...), custom_call_target="tpu_custom_call" | custom-call | flops 3221225472 | bytes 1048576 | tf_op jit(solution)/shard_map/middle1/pallas_call | solution.py:287
  21.4 3.1 %collective-permute-done.6.near.refs_2_ = bf16[2,512,128]{2,1,0:T(8,128)(2,1)S(1)} collective-permute-done((bf16[2,512,128]{2,1,0:T(8,128)(2,1)S(1)}, bf16[2,512,128]{2,1,0:T(8,128)(2,1)S(1)}, u32[]{:S(2)}, u32[]{:S(2)}) %collective-permute-start.6) | collective-permute-done | bytes 262176 | tf_op jit(solution)/shard_map/ppermute | solution.py:331
  24.5 0.0 collective-permute-start.7
  24.5 0.0 collective-permute-start.8
  24.5 1.5 %collective-permute-done.7.other.refs_3_ = bf16[2,512,128]{2,1,0:T(8,128)(2,1)S(1)} collective-permute-done((bf16[2,512,128]{2,1,0:T(8,128)(2,1)S(1)}, bf16[2,512,128]{2,1,0:T(8,128)(2,1)S(1)}, u32[]{:S(2)}, u32[]{:S(2)}) %collective-permute-start.7) | collective-permute-done | bytes 262176 | tf_op jit(solution)/shard_map/ppermute | solution.py:334
  26.0 3.0 %middle2.1 = (f32[8,384,128]{2,1,0:T(8,128)S(1)}, f32[8,384,128]{2,1,0:T(8,128)S(1)}, f32[128,128]{1,0:T(8,128)S(1)}) custom-call(bf16[128,1024]{1,0:T(8,128)(2,1)S(1)} %copy-done.1, bf16[1,256,1024]{2,1,0:T(8,128)(2,1)S(1)} %copy-done, ...), custom_call_target="tpu_custom_call", output_to_operand_aliasing={{0}: (5, {}), {1}: (6, {}), {2}: (7, {})} | custom-call | flops 3221225472 | bytes 1048576 | tf_op jit(solution)/shard_map/middle2/pallas_call | solution.py:287
  29.1 3.0 %collective-permute-done.8.near.refs_4_ = bf16[2,512,128]{2,1,0:T(8,128)(2,1)S(1)} collective-permute-done((bf16[2,512,128]{2,1,0:T(8,128)(2,1)S(1)}, bf16[2,512,128]{2,1,0:T(8,128)(2,1)S(1)}, u32[]{:S(2)}, u32[]{:S(2)}) %collective-permute-start.8) | collective-permute-done | bytes 262176 | tf_op jit(solution)/shard_map/ppermute | solution.py:331
  32.1 0.0 collective-permute-start.9
  32.1 0.0 collective-permute-start.10
  32.1 1.5 %collective-permute-done.9.other.refs_5_ = bf16[2,512,128]{2,1,0:T(8,128)(2,1)S(1)} collective-permute-done((bf16[2,512,128]{2,1,0:T(8,128)(2,1)S(1)}, bf16[2,512,128]{2,1,0:T(8,128)(2,1)S(1)}, u32[]{:S(2)}, u32[]{:S(2)}) %collective-permute-start.9) | collective-permute-done | bytes 262176 | tf_op jit(solution)/shard_map/ppermute | solution.py:334
  33.6 3.0 %middle3.1 = (f32[8,384,128]{2,1,0:T(8,128)S(1)}, f32[8,384,128]{2,1,0:T(8,128)S(1)}, f32[128,128]{1,0:T(8,128)S(1)}) custom-call(bf16[128,1024]{1,0:T(8,128)(2,1)S(1)} %copy-done.1, bf16[1,256,1024]{2,1,0:T(8,128)(2,1)S(1)} %copy-done, ...), custom_call_target="tpu_custom_call", output_to_operand_aliasing={{0}: (5, {}), {1}: (6, {}), {2}: (7, {})} | custom-call | flops 3221225472 | bytes 1048576 | tf_op jit(solution)/shard_map/middle3/pallas_call | solution.py:287
  36.7 3.0 %collective-permute-done.10.refs_6_ = bf16[2,512,128]{2,1,0:T(8,128)(2,1)S(1)} collective-permute-done((bf16[2,512,128]{2,1,0:T(8,128)(2,1)S(1)}, bf16[2,512,128]{2,1,0:T(8,128)(2,1)S(1)}, u32[]{:S(2)}, u32[]{:S(2)}) %collective-permute-start.10) | collective-permute-done | bytes 262176 | tf_op jit(solution)/shard_map/ppermute | solution.py:331
  39.7 37.4 %last.1 = bf16[8,48,1024]{2,1,0:T(8,128)(2,1)S(1)} custom-call(s32[8,128]{1,0:T(8,128)S(1)} %copy-done.2, bf16[128,1024]{1,0:T(8,128)(2,1)S(1)} %copy-done.1, bf16[1,256,1024]{2,1,0:T(8,128)(2,1)S(1)} %copy-done, bf16[2,512,128]{2,1,0:T(8,128)(2,1)S(1)} %constant_dynamic-update-slice_fusion.near.refs_0_, ...), custom_call_target="tpu_custom_call" | custom-call | flops 1610612736 | bytes 1048576 | tf_op jit(solution)/shard_map/last/pallas_call | solution.py:292
  77.1 18.9 %all_to_all.5.moved = bf16[8,48,1024]{2,1,0:T(8,128)(2,1)S(1)} all-to-all(bf16[8,48,1024]{2,1,0:T(8,128)(2,1)S(1)} %last.1), channel_id=1, replica_groups=mesh['group'=8,'ctx'=4,'head'=8] {'head'}, dimensions={0} | all-to-all | bytes 1572864 | tf_op jit(solution)/shard_map/all_to_all | solution.py:359
  95.9 1.0 %lay_out.1 = (bf16[16,8192]{1,0:T(8,128)(2,1)}, bf16[1,32,8192]{2,1,0:T(8,128)(2,1)}) custom-call(bf16[8,48,1024]{2,1,0:T(8,128)(2,1)S(1)} %all_to_all.5.moved), custom_call_target="tpu_custom_call" | custom-call | tf_op jit(solution)/shard_map/lay_out/pallas_call | solution.py:308
  (6 shorter events, 0.1 us)
Async XLA Ops:
  0.6 3.9 %collective-permute-start = (bf16[2,128,128]{2,1,0:T(8,128)(2,1)}, bf16[2,128,128]{2,1,0:T(8,128)(2,1)S(1)}, u32[]{:S(2)}, u32[]{:S(2)}) collective-permute-start(bf16[2,128,128]{2,1,0:T(8,128)(2,1)} %param.6), channel_id=1, source_target_pairs={{0,8},{8,0},{16,24},{24,16},{1,9},{9,1},{17,25},{25,17},{2,10},{10... | collective-permute-start | bytes 196616 | tf_op jit(solution)/shard_map/ppermute | solution.py:337
  0.7 6.2 %collective-permute-start.2 = (bf16[2,128,128]{2,1,0:T(8,128)(2,1)}, bf16[2,128,128]{2,1,0:T(8,128)(2,1)S(1)}, u32[]{:S(2)}, u32[]{:S(2)}) collective-permute-start(bf16[2,128,128]{2,1,0:T(8,128)(2,1)} %param.6), channel_id=1, source_target_pairs={{0,16},{16,0},{8,24},{24,8},{1,17},{17,1},{9,25},{25,9},{2,18},{18... | collective-permute-start | bytes 196616 | tf_op jit(solution)/shard_map/ppermute | solution.py:337
  3.1 4.3 %collective-permute-start.3 = (bf16[2,128,128]{2,1,0:T(8,128)(2,1)}, bf16[2,128,128]{2,1,0:T(8,128)(2,1)S(1)}, u32[]{:S(2)}, u32[]{:S(2)}) collective-permute-start(bf16[2,128,128]{2,1,0:T(8,128)(2,1)} %param.6), channel_id=1, source_target_pairs={{0,24},{24,0},{8,16},{16,8},{1,25},{25,1},{9,17},{17,9},{2,26},{26... | collective-permute-start | bytes 196616 | tf_op jit(solution)/shard_map/ppermute | solution.py:337
  3.8 0.8 copy-start.4
  3.8 1.1 %copy-start = (bf16[1,256,1024]{2,1,0:T(8,128)(2,1)S(1)}, bf16[1,256,1024]{2,1,0:T(8,128)(2,1)}, u32[]{:S(2)}) copy-start(bf16[1,256,1024]{2,1,0:T(8,128)(2,1)} %qc.11) | copy-start | bytes 1572868
  3.8 1.1 %copy-start.3 = (bf16[2,1,256,128]{3,2,1,0:T(8,128)(2,1)S(1)}, bf16[2,1,256,128]{3,2,1,0:T(8,128)(2,1)}, u32[]{:S(2)}) copy-start(bf16[2,1,256,128]{3,2,1,0:T(8,128)(2,1)} %kv.1) | copy-start | bytes 393220
  4.5 5.8 %copy-start.1 = (bf16[128,1024]{1,0:T(8,128)(2,1)S(1)}, bf16[128,1024]{1,0:T(8,128)(2,1)}, u32[]{:S(2)}) copy-start(bf16[128,1024]{1,0:T(8,128)(2,1)} %qp.9) | copy-start | bytes 786436
  4.9 0.7 copy-start.2
  7.4 9.3 %collective-permute-start.1 = (bf16[2,256,128]{2,1,0:T(8,128)(2,1)S(1)}, bf16[2,256,128]{2,1,0:T(8,128)(2,1)S(1)}, u32[]{:S(2)}, u32[]{:S(2)}) collective-permute-start(bf16[2,256,128]{2,1,0:T(8,128)(2,1)S(1)} %pad_maximum_fusion.1), channel_id=1, source_target_pairs={{0,32},{8,232},{16,48},{24,248},{32,64},{40,8},{48,80},{56,24},{64... | collective-permute-start | bytes 393224 | tf_op jit(solution)/shard_map/ppermute | solution.py:331
  8.4 8.3 %collective-permute-start.4 = (bf16[2,256,128]{2,1,0:T(8,128)(2,1)S(1)}, bf16[2,256,128]{2,1,0:T(8,128)(2,1)S(1)}, u32[]{:S(2)}, u32[]{:S(2)}) collective-permute-start(bf16[2,256,128]{2,1,0:T(8,128)(2,1)S(1)} %pad_maximum_fusion.2), channel_id=1, source_target_pairs={{0,32},{8,232},{16,48},{24,248},{32,64},{40,8},{48,80},{56,24},{64... | collective-permute-start | bytes 393224 | tf_op jit(solution)/shard_map/ppermute | solution.py:331
  16.8 1.6 %collective-permute-start.5 = (bf16[2,512,128]{2,1,0:T(8,128)(2,1)S(1)}, bf16[2,512,128]{2,1,0:T(8,128)(2,1)S(1)}, u32[]{:S(2)}, u32[]{:S(2)}) collective-permute-start(bf16[2,512,128]{2,1,0:T(8,128)(2,1)S(1)} %constant_dynamic-update-slice_fusion.near.refs_0_), channel_id=1, source_target_pairs={{0,8},{8,0},{16,24},{24,16},{1,9},{9,1},{17,25},{25,17},{2,10},{10... | collective-permute-start | bytes 786440 | tf_op jit(solution)/shard_map/ppermute | solution.py:334
  16.9 7.7 %collective-permute-start.6 = (bf16[2,512,128]{2,1,0:T(8,128)(2,1)S(1)}, bf16[2,512,128]{2,1,0:T(8,128)(2,1)S(1)}, u32[]{:S(2)}, u32[]{:S(2)}) collective-permute-start(bf16[2,512,128]{2,1,0:T(8,128)(2,1)S(1)} %constant_dynamic-update-slice_fusion.near.refs_0_), channel_id=1, source_target_pairs={{0,32},{8,232},{16,48},{24,248},{32,64},{40,8},{48,80},{56,24},{64... | collective-permute-start | bytes 786440 | tf_op jit(solution)/shard_map/ppermute | solution.py:331
  24.5 1.5 %collective-permute-start.7 = (bf16[2,512,128]{2,1,0:T(8,128)(2,1)S(1)}, bf16[2,512,128]{2,1,0:T(8,128)(2,1)S(1)}, u32[]{:S(2)}, u32[]{:S(2)}) collective-permute-start(bf16[2,512,128]{2,1,0:T(8,128)(2,1)S(1)} %collective-permute-done.6.near.refs_2_), channel_id=1, source_target_pairs={{0,8},{8,0},{16,24},{24,16},{1,9},{9,1},{17,25},{25,17},{2,10},{10... | collective-permute-start | bytes 786440 | tf_op jit(solution)/shard_map/ppermute | solution.py:334
  24.5 7.6 %collective-permute-start.8 = (bf16[2,512,128]{2,1,0:T(8,128)(2,1)S(1)}, bf16[2,512,128]{2,1,0:T(8,128)(2,1)S(1)}, u32[]{:S(2)}, u32[]{:S(2)}) collective-permute-start(bf16[2,512,128]{2,1,0:T(8,128)(2,1)S(1)} %collective-permute-done.6.near.refs_2_), channel_id=1, source_target_pairs={{0,32},{8,232},{16,48},{24,248},{32,64},{40,8},{48,80},{56,24},{64... | collective-permute-start | bytes 786440 | tf_op jit(solution)/shard_map/ppermute | solution.py:331
  32.1 1.5 %collective-permute-start.9 = (bf16[2,512,128]{2,1,0:T(8,128)(2,1)S(1)}, bf16[2,512,128]{2,1,0:T(8,128)(2,1)S(1)}, u32[]{:S(2)}, u32[]{:S(2)}) collective-permute-start(bf16[2,512,128]{2,1,0:T(8,128)(2,1)S(1)} %collective-permute-done.8.near.refs_4_), channel_id=1, source_target_pairs={{0,8},{8,0},{16,24},{24,16},{1,9},{9,1},{17,25},{25,17},{2,10},{10... | collective-permute-start | bytes 786440 | tf_op jit(solution)/shard_map/ppermute | solution.py:334
  32.1 7.6 %collective-permute-start.10 = (bf16[2,512,128]{2,1,0:T(8,128)(2,1)S(1)}, bf16[2,512,128]{2,1,0:T(8,128)(2,1)S(1)}, u32[]{:S(2)}, u32[]{:S(2)}) collective-permute-start(bf16[2,512,128]{2,1,0:T(8,128)(2,1)S(1)} %collective-permute-done.8.near.refs_4_), channel_id=1, source_target_pairs={{0,32},{8,232},{16,48},{24,248},{32,64},{40,8},{48,80},{56,24},{64... | collective-permute-start | bytes 786440 | tf_op jit(solution)/shard_map/ppermute | solution.py:331
